TPU v7x, 128 devices: a whole 4x4x4 slice. The times are simulated.
128 devices in a mesh: dp: 32 (over x_lo, z, y), mp: 4 (over x_hi, core).
Axes of the slice: x: 4 (x_hi: 2, x_lo: 2; x = x_hi * 2 + x_lo), y: 4, z: 4, core: 2. Of those that a mesh axis runs over, the one named last changes fastest.
Arguments:
- tokens: bfloat16 [16384, 2048], P(('dp', 'mp')), may hold values from -6 to 6
- cotangent: bfloat16 [16384, 2048], P(('dp', 'mp')), may hold values from -7.5 to 7.5
- doc_lengths: int32 [32, 4], P('dp'), may hold values from 1 to 385, 512 in all within a row
- row_owner: int32 [32], replicated, may hold values from 0 to 31, each once
- norm_params: float32 [2, 2048], replicated, may hold values from -1.2 to 1.75, as said below
- norm_moment1: float32 [2, 2048], replicated
- norm_moment2: float32 [2, 2048], replicated, as said below
- qkv_weight: float32 [2048, 6144], P('dp', 'mp'), may hold values from -0.125 to 0.125
- out_weight: float32 [2048, 2048], P('dp', 'mp')
- gate_weight: float32 [2048, 5632], P('dp', 'mp'), may hold values from -0.125 to 0.125
- up_weight: float32 [2048, 5632], P('dp', 'mp'), may hold values from -0.125 to 0.125
- down_weight: float32 [2048, 5632], P('dp', 'mp')
- qkv_moment1: float32 [2048, 6144], P('dp', 'mp')
- out_moment1: float32 [2048, 2048], P('dp', 'mp')
- gate_moment1: float32 [2048, 5632], P('dp', 'mp')
- up_moment1: float32 [2048, 5632], P('dp', 'mp')
- down_moment1: float32 [2048, 5632], P('dp', 'mp')
- qkv_moment2: float32 [2048, 6144], P('dp', 'mp'), as said below
- out_moment2: float32 [2048, 2048], P('dp', 'mp'), as said below
- gate_moment2: float32 [2048, 5632], P('dp', 'mp'), as said below
- up_moment2: float32 [2048, 5632], P('dp', 'mp'), as said below
- down_moment2: float32 [2048, 5632], P('dp', 'mp'), as said below
- qkv_basis: float32 [48, 128, 128], P('mp'), may hold values from -0.5 to 0.5
- out_basis: float32 [16, 128, 128], P('mp'), may hold values from -0.5 to 0.5
- gate_basis: float32 [44, 128, 128], P('mp'), may hold values from -0.5 to 0.5
- up_basis: float32 [44, 128, 128], P('mp'), may hold values from -0.5 to 0.5
- down_basis: float32 [44, 128, 128], P('mp'), may hold values from -0.5 to 0.5
Outputs:
- out: bfloat16 [16384, 2048], P(('dp', 'mp'))
- input_grad: bfloat16 [16384, 2048], P(('dp', 'mp'))
- grad_norm: float32 [], replicated
- norm_grads: float32 [2, 2048], replicated
- norm_moment1_new: float32 [2, 2048], replicated
- norm_moment2_new: float32 [2, 2048], replicated
- norm_params_new: float32 [2, 2048], replicated
- qkv_grad: float32 [2048, 6144], P('dp', 'mp')
- out_grad: float32 [2048, 2048], P('dp', 'mp')
- gate_grad: float32 [2048, 5632], P('dp', 'mp')
- up_grad: float32 [2048, 5632], P('dp', 'mp')
- down_grad: float32 [2048, 5632], P('dp', 'mp')
- qkv_moment1_new: float32 [2048, 6144], P('dp', 'mp')
- out_moment1_new: float32 [2048, 2048], P('dp', 'mp')
- gate_moment1_new: float32 [2048, 5632], P('dp', 'mp')
- up_moment1_new: float32 [2048, 5632], P('dp', 'mp')
- down_moment1_new: float32 [2048, 5632], P('dp', 'mp')
- qkv_moment2_new: float32 [2048, 6144], P('dp', 'mp')
- out_moment2_new: float32 [2048, 2048], P('dp', 'mp')
- gate_moment2_new: float32 [2048, 5632], P('dp', 'mp')
- up_moment2_new: float32 [2048, 5632], P('dp', 'mp')
- down_moment2_new: float32 [2048, 5632], P('dp', 'mp')
- qkv_new: float32 [2048, 6144], P('dp', 'mp')
- out_new: float32 [2048, 2048], P('dp', 'mp')
- gate_new: float32 [2048, 5632], P('dp', 'mp')
- up_new: float32 [2048, 5632], P('dp', 'mp')
- down_new: float32 [2048, 5632], P('dp', 'mp')
Inputs may be any that keep to these rules, and one draw needn't show every extreme that they name: `doc_lengths`: one document of each sequence has exactly 385 tokens. `row_owner`: each value once. `norm_params`: gains positive. `norm_moment2`: positive. `qkv_moment2`: positive. `out_moment2`: positive. `gate_moment2`: positive. `up_moment2`: positive. `down_moment2`: positive.
All inputs are finite; a program needn't handle non-finite values.
Results may differ from a plain program's by a relative error of at most 0.005.
The roundings to bfloat16 on the way count: a program that leaves them out, or rounds other values in their place, can miss the bound.
Values may be sent and summed in bfloat16 or wider, within the bound.
A program may use at most 256 MiB of HBM per device.

v0:
```python
import math

import jax
import jax.numpy as jnp
from jax import lax
from jax.sharding import PartitionSpec as P

HEAD_DIM = 64
ROT = 16
STEP = 5


NORM_EPSILON = 1e-05
BETA_ONE = 0.5
BETA_TWO = 0.5
ADAM_EPS = 1e-08
WEIGHT_DECAY = 0.01
RATE_LIST = (0.02, 0.1, 0.02, 0.02, 0.015)
NORM_RATE = 0.2
CLIP_LIMIT = 1.0
MASK_FILL = -1e30
PRECISE = lax.Precision.HIGHEST
ROWS_DIMS = (((0,), (0,)), ((), ()))
COLS_DIMS = (((1,), (1,)), ((), ()))


def doc_layout(lengths, total):
    ends = jnp.cumsum(lengths)
    index = jnp.arange(total, dtype=jnp.int32)
    passed = (index[:, None] >= ends[None, :]).astype(jnp.int32)
    doc_ids = jnp.sum(passed, 1)
    starts = jnp.sum(passed * lengths[None, :], 1)
    return (doc_ids, index - starts, index)


def turn_angles(positions):
    half = ROT // 2
    freq = 10000.0 ** (-2.0 * jnp.arange(half, dtype=jnp.float32) / ROT)
    angle = positions.astype(jnp.float32)[:, None] * freq[None, :]
    return (jnp.cos(angle)[:, None, :], jnp.sin(angle)[:, None, :])


def rotate(field, cosine, sine):
    half = ROT // 2
    lead_half = field[..., :half]
    tail_half = field[..., half:ROT]
    return jnp.concatenate(
        [
            lead_half * cosine - tail_half * sine,
            tail_half * cosine + lead_half * sine,
            field[..., ROT:],
        ],
        -1,
    )


def unrotate(field, cosine, sine):
    half = ROT // 2
    lead_half = field[..., :half]
    tail_half = field[..., half:ROT]
    return jnp.concatenate(
        [
            lead_half * cosine + tail_half * sine,
            tail_half * cosine - lead_half * sine,
            field[..., ROT:],
        ],
        -1,
    )


def block_order(weight, order, owners):
    return weight.reshape(owners, -1, weight.shape[1])[order].reshape(-1, weight.shape[1])


def soap_update(weight, grad, first, second, basis, rate):
    rows, cols = grad.shape
    blocks = basis.shape[0]
    turned = jnp.einsum(
        "rbi,bij->rbj", grad.reshape(rows, blocks, -1), basis, precision=PRECISE
    ).reshape(rows, cols)
    first_new = BETA_ONE * first + (1.0 - BETA_ONE) * turned
    second_new = BETA_TWO * second + (1.0 - BETA_TWO) * turned * turned
    ratio = (
        first_new
        / (1.0 - BETA_ONE**STEP)
        / (jnp.sqrt(second_new / (1.0 - BETA_TWO**STEP)) + ADAM_EPS)
    )
    back = jnp.einsum(
        "rbj,bij->rbi", ratio.reshape(rows, blocks, -1), basis, precision=PRECISE
    ).reshape(rows, cols)
    return (first_new, second_new, weight - rate * (back + WEIGHT_DECAY * weight))


def adam_plain(param, grad, first, second, rate):
    first_new = BETA_ONE * first + (1.0 - BETA_ONE) * grad
    second_new = BETA_TWO * second + (1.0 - BETA_TWO) * grad * grad
    ratio = (
        first_new
        / (1.0 - BETA_ONE**STEP)
        / (jnp.sqrt(second_new / (1.0 - BETA_TWO**STEP)) + ADAM_EPS)
    )
    return (first_new, second_new, param - rate * ratio)


def body(
    tokens,
    cotangent,
    doc_lengths,
    row_owner,
    norm_params,
    norm_moment1,
    norm_moment2,
    qkv_weight,
    out_weight,
    gate_weight,
    up_weight,
    down_weight,
    qkv_moment1,
    out_moment1,
    gate_moment1,
    up_moment1,
    down_moment1,
    qkv_moment2,
    out_moment2,
    gate_moment2,
    up_moment2,
    down_moment2,
    qkv_basis,
    out_basis,
    gate_basis,
    up_basis,
    down_basis,
):
    owners = lax.axis_size("dp")
    stored_copies = (
        lax.all_gather(qkv_weight.astype(jnp.bfloat16), "dp", axis=0, tiled=True),
        lax.all_gather(out_weight.astype(jnp.bfloat16), "dp", axis=0, tiled=True),
        lax.all_gather(gate_weight.astype(jnp.bfloat16), "dp", axis=0, tiled=True),
        lax.all_gather(up_weight.astype(jnp.bfloat16), "dp", axis=0, tiled=True),
        lax.all_gather(down_weight.astype(jnp.bfloat16), "dp", axis=0, tiled=True),
    )
    qkv_copy, out_copy, gate_copy, up_copy, down_copy = [
        block_order(item, row_owner, owners) for item in stored_copies
    ]
    inputs = tokens.astype(jnp.float32)
    norm_gain = norm_params[0]
    norm_shift = norm_params[1]
    row_mean = jnp.mean(inputs, -1, keepdims=True)
    centered_input = inputs - row_mean
    row_variance = jnp.mean(centered_input * centered_input, -1, keepdims=True)
    inverse_deviation = lax.rsqrt(row_variance + NORM_EPSILON)
    standardized_input = centered_input * inverse_deviation
    normed_output = (standardized_input * norm_gain + norm_shift).astype(jnp.bfloat16)
    normed_all = lax.all_gather(normed_output, "mp", axis=0, tiled=True)
    length = normed_all.shape[0]
    doc_ids, positions, index = doc_layout(doc_lengths[0], length)
    cosine, sine = turn_angles(positions)
    heads_local = qkv_copy.shape[1] // (3 * HEAD_DIM)
    scale = 1.0 / math.sqrt(HEAD_DIM)
    qkv_pre = jnp.dot(normed_all, qkv_copy, preferred_element_type=jnp.float32).reshape(
        length, heads_local, 3, HEAD_DIM
    )
    queries = (rotate(qkv_pre[:, :, 0], cosine, sine) * scale).astype(jnp.bfloat16)
    key_rows = rotate(qkv_pre[:, :, 1], cosine, sine).astype(jnp.bfloat16)
    value_rows = qkv_pre[:, :, 2].astype(jnp.bfloat16)
    block_rows = min(512, length)
    block_count = length // block_rows
    query_blocks = queries.reshape(block_count, block_rows, heads_local, HEAD_DIM)
    doc_blocks = doc_ids.reshape(block_count, block_rows)
    index_blocks = index.reshape(block_count, block_rows)

    def allowed_mask(block_docs, block_index):
        return (block_docs[:, None] == doc_ids[None, :]) & (block_index[:, None] >= index[None, :])

    def attend(packed):
        block_query, block_docs, block_index = packed
        scores = jnp.einsum(
            "qhd,khd->hqk", block_query, key_rows, preferred_element_type=jnp.float32
        )
        scores = jnp.where(allowed_mask(block_docs, block_index)[None], scores, MASK_FILL)
        peak = jnp.max(scores, -1, keepdims=True)
        expo = jnp.exp(scores - peak)
        total = jnp.sum(expo, -1, keepdims=True)
        attn_probs = (expo / total).astype(jnp.bfloat16)
        mixed = jnp.einsum(
            "hqk,khd->qhd", attn_probs, value_rows, preferred_element_type=jnp.float32
        )
        return (mixed, peak + jnp.log(total))

    attn_out, log_totals = lax.map(attend, (query_blocks, doc_blocks, index_blocks))
    attn_low = attn_out.reshape(length, heads_local * HEAD_DIM).astype(jnp.bfloat16)
    gate_pre = jnp.dot(normed_all, gate_copy, preferred_element_type=jnp.float32)
    up_pre = jnp.dot(normed_all, up_copy, preferred_element_type=jnp.float32)
    sigma = jax.nn.sigmoid(gate_pre)
    hidden = (gate_pre * sigma * up_pre).astype(jnp.bfloat16)
    branch = lax.psum_scatter(
        lax.dot_general(attn_low, out_copy, COLS_DIMS, preferred_element_type=jnp.float32)
        + lax.dot_general(hidden, down_copy, COLS_DIMS, preferred_element_type=jnp.float32),
        "mp",
        scatter_dimension=0,
        tiled=True,
    )
    out = (inputs + branch).astype(jnp.bfloat16)
    grad_all = lax.all_gather(cotangent, "mp", axis=0, tiled=True)
    out_full = lax.dot_general(grad_all, attn_low, ROWS_DIMS, preferred_element_type=jnp.float32)
    down_full = lax.dot_general(grad_all, hidden, ROWS_DIMS, preferred_element_type=jnp.float32)
    d_attn = jnp.dot(grad_all, out_copy, preferred_element_type=jnp.float32).astype(jnp.bfloat16)
    d_hidden = jnp.dot(grad_all, down_copy, preferred_element_type=jnp.float32)
    d_gate = (d_hidden * up_pre * sigma * (1.0 + gate_pre * (1.0 - sigma))).astype(jnp.bfloat16)
    d_up = (d_hidden * gate_pre * sigma).astype(jnp.bfloat16)
    d_attn_blocks = d_attn.reshape(block_count, block_rows, heads_local, HEAD_DIM)

    def attend_back(carry, packed):
        key_sum, value_sum = carry
        block_query, block_grad, block_log, block_docs, block_index = packed
        scores = jnp.einsum(
            "qhd,khd->hqk", block_query, key_rows, preferred_element_type=jnp.float32
        )
        prob_full = jnp.where(
            allowed_mask(block_docs, block_index)[None], jnp.exp(scores - block_log), 0.0
        )
        attn_probs = prob_full.astype(jnp.bfloat16)
        d_prob = jnp.einsum(
            "qhd,khd->hqk", block_grad, value_rows, preferred_element_type=jnp.float32
        )
        delta = jnp.sum(prob_full * d_prob, -1, keepdims=True)
        d_score = (prob_full * (d_prob - delta)).astype(jnp.bfloat16)
        d_query = jnp.einsum("hqk,khd->qhd", d_score, key_rows, preferred_element_type=jnp.float32)
        key_sum = key_sum + jnp.einsum(
            "hqk,qhd->khd", d_score, block_query, preferred_element_type=jnp.float32
        )
        value_sum = value_sum + jnp.einsum(
            "hqk,qhd->khd", attn_probs, block_grad, preferred_element_type=jnp.float32
        )
        return ((key_sum, value_sum), d_query)

    zero_heads = jnp.zeros((length, heads_local, HEAD_DIM), jnp.float32)
    (d_keys, d_values), d_queries = lax.scan(
        attend_back,
        (zero_heads, zero_heads),
        (query_blocks, d_attn_blocks, log_totals, doc_blocks, index_blocks),
    )
    d_queries = d_queries.reshape(length, heads_local, HEAD_DIM) * scale
    d_qkv = jnp.stack(
        [unrotate(d_queries, cosine, sine), unrotate(d_keys, cosine, sine), d_values], 2
    )
    d_qkv = d_qkv.reshape(length, heads_local * 3 * HEAD_DIM).astype(jnp.bfloat16)
    qkv_full = lax.dot_general(normed_all, d_qkv, ROWS_DIMS, preferred_element_type=jnp.float32)
    gate_full = lax.dot_general(normed_all, d_gate, ROWS_DIMS, preferred_element_type=jnp.float32)
    up_full = lax.dot_general(normed_all, d_up, ROWS_DIMS, preferred_element_type=jnp.float32)
    normed_cotangent = lax.psum_scatter(
        lax.dot_general(d_qkv, qkv_copy, COLS_DIMS, preferred_element_type=jnp.float32)
        + lax.dot_general(d_gate, gate_copy, COLS_DIMS, preferred_element_type=jnp.float32)
        + lax.dot_general(d_up, up_copy, COLS_DIMS, preferred_element_type=jnp.float32),
        "mp",
        scatter_dimension=0,
        tiled=True,
    )
    norm_partial_terms = jnp.stack(
        [jnp.sum(normed_cotangent * standardized_input, 0), jnp.sum(normed_cotangent, 0)]
    )
    standardized_cotangent = normed_cotangent * norm_gain
    input_grad = (
        cotangent.astype(jnp.float32)
        + inverse_deviation
        * (
            standardized_cotangent
            - jnp.mean(standardized_cotangent, -1, keepdims=True)
            - standardized_input
            * jnp.mean(standardized_cotangent * standardized_input, -1, keepdims=True)
        )
    ).astype(jnp.bfloat16)
    norm_raw = lax.psum(norm_partial_terms, ("dp", "mp"))
    inverse = jnp.argsort(row_owner)
    owned = (
        lax.psum_scatter(
            block_order(qkv_full, inverse, owners), "dp", scatter_dimension=0, tiled=True
        ),
        lax.psum_scatter(
            block_order(out_full, inverse, owners), "dp", scatter_dimension=0, tiled=True
        ),
        lax.psum_scatter(
            block_order(gate_full, inverse, owners), "dp", scatter_dimension=0, tiled=True
        ),
        lax.psum_scatter(
            block_order(up_full, inverse, owners), "dp", scatter_dimension=0, tiled=True
        ),
        lax.psum_scatter(
            block_order(down_full, inverse, owners), "dp", scatter_dimension=0, tiled=True
        ),
    )
    squares = jnp.sum(owned[0] * owned[0])
    for grad in owned[1:]:
        squares = squares + jnp.sum(grad * grad)
    square_total = lax.psum(squares, ("dp", "mp"))
    grad_norm = jnp.sqrt(square_total + jnp.sum(norm_raw * norm_raw))
    clip = jnp.minimum(1.0, CLIP_LIMIT / grad_norm)
    norm_grads = clip * norm_raw
    norm_first, norm_second, norm_new = adam_plain(
        norm_params, norm_grads, norm_moment1, norm_moment2, NORM_RATE
    )
    masters = (qkv_weight, out_weight, gate_weight, up_weight, down_weight)
    firsts = (qkv_moment1, out_moment1, gate_moment1, up_moment1, down_moment1)
    seconds = (qkv_moment2, out_moment2, gate_moment2, up_moment2, down_moment2)
    bases = (qkv_basis, out_basis, gate_basis, up_basis, down_basis)
    clipped = [clip * grad for grad in owned]
    updates = [
        soap_update(masters[i], clipped[i], firsts[i], seconds[i], bases[i], RATE_LIST[i])
        for i in range(5)
    ]
    return (
        out,
        input_grad,
        grad_norm,
        norm_grads,
        norm_first,
        norm_second,
        norm_new,
        clipped[0],
        clipped[1],
        clipped[2],
        clipped[3],
        clipped[4],
        updates[0][0],
        updates[1][0],
        updates[2][0],
        updates[3][0],
        updates[4][0],
        updates[0][1],
        updates[1][1],
        updates[2][1],
        updates[3][1],
        updates[4][1],
        updates[0][2],
        updates[1][2],
        updates[2][2],
        updates[3][2],
        updates[4][2],
    )


def solution(mesh):
    in_specs = (
        P(("dp", "mp"), None),
        P(("dp", "mp"), None),
        P("dp", None),
        P(),
        P(),
        P(),
        P(),
        P("dp", "mp"),
        P("dp", "mp"),
        P("dp", "mp"),
        P("dp", "mp"),
        P("dp", "mp"),
        P("dp", "mp"),
        P("dp", "mp"),
        P("dp", "mp"),
        P("dp", "mp"),
        P("dp", "mp"),
        P("dp", "mp"),
        P("dp", "mp"),
        P("dp", "mp"),
        P("dp", "mp"),
        P("dp", "mp"),
        P("mp", None, None),
        P("mp", None, None),
        P("mp", None, None),
        P("mp", None, None),
        P("mp", None, None),
    )
    out_specs = (
        P(("dp", "mp"), None),
        P(("dp", "mp"), None),
        P(),
        P(),
        P(),
        P(),
        P(),
        P("dp", "mp"),
        P("dp", "mp"),
        P("dp", "mp"),
        P("dp", "mp"),
        P("dp", "mp"),
        P("dp", "mp"),
        P("dp", "mp"),
        P("dp", "mp"),
        P("dp", "mp"),
        P("dp", "mp"),
        P("dp", "mp"),
        P("dp", "mp"),
        P("dp", "mp"),
        P("dp", "mp"),
        P("dp", "mp"),
        P("dp", "mp"),
        P("dp", "mp"),
        P("dp", "mp"),
        P("dp", "mp"),
        P("dp", "mp"),
    )
    return jax.shard_map(body, mesh=mesh, in_specs=in_specs, out_specs=out_specs, check_vma=False)
```

profile of v0, /device:TPU:1, one launch (start us, length us, event | category | flops | bytes accessed | tf_op | source)
XLA Modules:
  0.0 2055.7 jit_solution(9933430608371308273)
XLA Ops:
  24.6 121.8 %all-gather.12.cloned.1.call-done = bf16[2048,512]{1,0:T(8,128)(2,1)} async-done(((bf16[64,512]{1,0:T(8,128)(2,1)}), bf16[2048,512]{1,0:T(8,128)(2,1)}) %all-gather.12.cloned.1.call-update) | async-done | bytes 2097168 | tf_op jit(solution)/shard_map/all_gather | solution.py:137
  148.6 47.0 %all-gather.20.cloned.1.call-done = bf16[512,2048]{1,0:T(8,128)(2,1)} async-done(((bf16[128,2048]{1,0:T(8,128)(2,1)}), bf16[512,2048]{1,0:T(8,128)(2,1)}) %all-gather.20.cloned.1.call-update) | async-done | bytes 2097168 | tf_op jit(solution)/shard_map/all_gather | solution.py:204
  199.3 141.4 %all-gather.14.cloned.1.call-done = bf16[2048,1408]{1,0:T(8,128)(2,1)} async-done(((bf16[64,1408]{1,0:T(8,128)(2,1)}), bf16[2048,1408]{1,0:T(8,128)(2,1)}) %all-gather.14.cloned.1.call-update) | async-done | bytes 5767184 | tf_op jit(solution)/shard_map/all_gather | solution.py:138
  347.0 158.3 %all-gather.16.cloned.1.call-done = bf16[2048,1408]{1,0:T(8,128)(2,1)} async-done(((bf16[64,1408]{1,0:T(8,128)(2,1)}), bf16[2048,1408]{1,0:T(8,128)(2,1)}) %all-gather.16.cloned.1.call-update) | async-done | bytes 5767184 | tf_op jit(solution)/shard_map/all_gather | solution.py:139
  511.5 158.3 %all-gather.18.cloned.1.call-done = bf16[2048,1408]{1,0:T(8,128)(2,1)} async-done(((bf16[64,1408]{1,0:T(8,128)(2,1)}), bf16[2048,1408]{1,0:T(8,128)(2,1)}) %all-gather.18.cloned.1.call-update) | async-done | bytes 5767184 | tf_op jit(solution)/shard_map/all_gather | solution.py:140
  676.1 41.5 %all-gather.8.cloned.1.call-done = bf16[512,2048]{1,0:T(8,128)(2,1)} async-done(((bf16[128,2048]{1,0:T(8,128)(2,1)}), bf16[512,2048]{1,0:T(8,128)(2,1)}) %all-gather.8.cloned.1.call-update) | async-done | bytes 2097168 | tf_op jit(solution)/shard_map/all_gather | solution.py:154
  717.6 8.2 fusion.91
  725.9 137.9 %all-gather.10.cloned.1.call-done = bf16[2048,1536]{1,0:T(8,128)(2,1)} async-done(((bf16[64,1536]{1,0:T(8,128)(2,1)}), bf16[2048,1536]{1,0:T(8,128)(2,1)}) %all-gather.10.cloned.1.call-update) | async-done | bytes 6291472 | tf_op jit(solution)/shard_map/all_gather | solution.py:136
  870.2 9.3 copy.106
  913.4 8.2 multiply_convert_fusion.1
  960.4 11.9 copy.117
  972.3 9.9 gather_fusion.9
  991.3 9.9 gather_fusion.8
  1008.9 9.9 gather_fusion.7
  1021.7 10.1 fusion.95
  1031.8 10.5 gather_fusion.5
  1052.0 20.1 reduce-scatter.14.cloned.1.call-done
  1073.6 70.7 %reduce-scatter.10.cloned.1.call-done = f32[128,2048]{1,0:T(8,128)} async-done(((f32[512,2048]{1,0:T(8,128)}), f32[128,2048]{1,0:T(8,128)}) %reduce-scatter.10.cloned.1.call-update) | async-done | bytes 1048592 | tf_op jit(solution)/shard_map/reduce_scatter | solution.py:251
  1146.0 165.4 %reduce-scatter.20.cloned.1.call-done = f32[64,1408]{1,0:T(8,128)} async-done(((f32[2048,1408]{1,0:T(8,128)}), f32[64,1408]{1,0:T(8,128)}) %reduce-scatter.20.cloned.1.call-update) | async-done | bytes 360464 | tf_op jit(solution)/shard_map/reduce_scatter | solution.py:288
  1313.1 185.4 %reduce-scatter.18.cloned.1.call-done = f32[64,1408]{1,0:T(8,128)} async-done(((f32[2048,1408]{1,0:T(8,128)}), f32[64,1408]{1,0:T(8,128)}) %reduce-scatter.18.cloned.1.call-update) | async-done | bytes 360464 | tf_op jit(solution)/shard_map/reduce_scatter | solution.py:285
  1500.2 185.0 %reduce-scatter.16.cloned.1.call-done = f32[64,1408]{1,0:T(8,128)} async-done(((f32[2048,1408]{1,0:T(8,128)}), f32[64,1408]{1,0:T(8,128)}) %reduce-scatter.16.cloned.1.call-update) | async-done | bytes 360464 | tf_op jit(solution)/shard_map/reduce_scatter | solution.py:282
  1686.9 187.9 %reduce-scatter.12.cloned.1.call-done = f32[64,1536]{1,0:T(8,128)} async-done(((f32[2048,1536]{1,0:T(8,128)}), f32[64,1536]{1,0:T(8,128)}) %reduce-scatter.12.cloned.1.call-update) | async-done | bytes 393232 | tf_op jit(solution)/shard_map/reduce_scatter | solution.py:276
  1879.7 68.9 %reduce-scatter.8.cloned.1.call-done = f32[128,2048]{1,0:T(8,128)} async-done(((f32[512,2048]{1,0:T(8,128)}), f32[128,2048]{1,0:T(8,128)}) %reduce-scatter.8.cloned.1.call-update) | async-done | bytes 1048592 | tf_op jit(solution)/shard_map/reduce_scatter | solution.py:196
  1951.7 65.4 %all-reduce = (f32[]{:T(128)}, f32[2,2048]{1,0:T(2,128)S(1)}) all-reduce(f32[]{:T(128)S(6)} %add.218, f32[2,2048]{1,0:T(2,128)S(1)} %pad_maximum_fusion.4), channel_id=1, replica_groups=mesh['dp'=32,'mp'=4] {'dp','mp'}, use_global_device_ids=true, to_apply=%region_23.24 | all-reduce | flops 4097 | bytes 32776 | tf_op jit(solution)/shard_map/psum | solution.py:295
  (263 shorter events, 192.2 us)
Async XLA Ops:
  7.2 2031.8 %copy-start = (f32[12,128,128]{2,1,0:T(8,128)S(1)}, f32[12,128,128]{2,1,0:T(8,128)}, u32[]{:S(2)}) copy-start(f32[12,128,128]{2,1,0:T(8,128)} %param.49) | copy-start | bytes 2359300
  7.3 139.1 %all-gather.12.cloned.1.call-start = ((), (), s32[]{:S(2)}) async-start(), calls=%async_computation.9 | async-start | bytes 2162688 | tf_op jit(solution)/shard_map/all_gather | solution.py:137
  9.0 186.6 %all-gather.20.cloned.1.call-start = ((), (), s32[]{:S(2)}) async-start(), calls=%async_computation.14 | async-start | bytes 2621440 | tf_op jit(solution)/shard_map/all_gather | solution.py:204
  9.7 331.0 %all-gather.14.cloned.1.call-start = ((), (), s32[]{:S(2)}) async-start(), calls=%async_computation.10 | async-start | bytes 5947392 | tf_op jit(solution)/shard_map/all_gather | solution.py:138
  11.5 493.8 %all-gather.16.cloned.1.call-start = ((), (), s32[]{:S(2)}) async-start(), calls=%async_computation.11 | async-start | bytes 5947392 | tf_op jit(solution)/shard_map/all_gather | solution.py:139
  13.2 656.6 %all-gather.18.cloned.1.call-start = ((), (), s32[]{:S(2)}) async-start(), calls=%async_computation.12 | async-start | bytes 5947392 | tf_op jit(solution)/shard_map/all_gather | solution.py:140
  15.0 702.6 %all-gather.8.cloned.1.call-start = ((), (), s32[]{:S(2)}) async-start(), calls=%async_computation.7 | async-start | bytes 2621440 | tf_op jit(solution)/shard_map/all_gather | solution.py:154
  20.2 843.5 %all-gather.10.cloned.1.call-start = ((), (), s32[]{:S(2)}) async-start(), calls=%async_computation.8 | async-start | bytes 6488064 | tf_op jit(solution)/shard_map/all_gather | solution.py:136
  21.0 1051.0 %reduce-scatter.14.cloned.1.call-start = ((), (), s32[]{:S(2)}) async-start(), calls=%async_computation.17 | async-start | bytes 4325376 | tf_op jit(solution)/shard_map/reduce_scatter | solution.py:279
  148.6 198.4 %copy-start.4 = (bf16[32,64,512]{2,1,0:T(8,128)(2,1)}, bf16[32,64,512]{2,1,0:T(8,128)(2,1)S(1)}, u32[]{:S(2)}) copy-start(bf16[32,64,512]{2,1,0:T(8,128)(2,1)S(1)} %gather_fusion.1) | copy-start | bytes 6291460
  906.6 237.6 %reduce-scatter.10.cloned.1.call-start = ((), (), s32[]{:S(2)}) async-start(), calls=%async_computation.15 | async-start | bytes 5242880 | tf_op jit(solution)/shard_map/reduce_scatter | solution.py:251
  951.6 359.8 %reduce-scatter.20.cloned.1.call-start = ((), (), s32[]{:S(2)}) async-start(), calls=%async_computation.20 | async-start | bytes 11894784 | tf_op jit(solution)/shard_map/reduce_scatter | solution.py:288
  982.2 516.3 %reduce-scatter.18.cloned.1.call-start = ((), (), s32[]{:S(2)}) async-start(), calls=%async_computation.19 | async-start | bytes 11894784 | tf_op jit(solution)/shard_map/reduce_scatter | solution.py:285
  1001.3 684.0 %reduce-scatter.16.cloned.1.call-start = ((), (), s32[]{:S(2)}) async-start(), calls=%async_computation.18 | async-start | bytes 11894784 | tf_op jit(solution)/shard_map/reduce_scatter | solution.py:282
  1018.7 856.1 %reduce-scatter.12.cloned.1.call-start = ((), (), s32[]{:S(2)}) async-start(), calls=%async_computation.16 | async-start | bytes 12976128 | tf_op jit(solution)/shard_map/reduce_scatter | solution.py:276
  1042.3 906.3 %reduce-scatter.8.cloned.1.call-start = ((), (), s32[]{:S(2)}) async-start(), calls=%async_computation.13 | async-start | bytes 5242880 | tf_op jit(solution)/shard_map/reduce_scatter | solution.py:196
  1051.9 92.3 %copy-start.3 = (bf16[128,2048]{1,0:T(8,128)(2,1)S(1)}, bf16[128,2048]{1,0:T(8,128)(2,1)}, u32[]{:S(2)}) copy-start(bf16[128,2048]{1,0:T(8,128)(2,1)} %param.27) | copy-start | bytes 1572868
  1051.9 92.3 %copy-start.43 = (f32[1,2048]{1,0:T(1,128)S(1)}, f32[1,2048]{1,0:T(1,128)}, u32[]{:S(2)}) copy-start(f32[1,2048]{1,0:T(1,128)} %copy-done.42) | copy-start | bytes 24580
  1051.9 92.3 %copy-start.49 = (f32[128]{0:T(128)S(1)}, f32[128]{0:T(128)}, u32[]{:S(2)}) copy-start(f32[128]{0:T(128)} %copy-done.48) | copy-start | bytes 1540
  1051.9 92.3 %copy-start.51 = (f32[128]{0:T(128)S(1)}, f32[128]{0:T(128)}, u32[]{:S(2)}) copy-start(f32[128]{0:T(128)} %copy-done.50) | copy-start | bytes 1540
  1051.9 896.7 %copy-start.19 = (bf16[128,2048]{1,0:T(8,128)(2,1)S(1)}, bf16[128,2048]{1,0:T(8,128)(2,1)}, u32[]{:S(2)}) copy-start(bf16[128,2048]{1,0:T(8,128)(2,1)} %param.28) | copy-start | bytes 1572868
  1146.0 879.5 %copy-start.11 = (f32[11,128,128]{2,1,0:T(8,128)S(1)}, f32[11,128,128]{2,1,0:T(8,128)}, u32[]{:S(2)}) copy-start(f32[11,128,128]{2,1,0:T(8,128)} %param.53) | copy-start | bytes 2162692
  1311.4 714.1 %copy-start.7 = (f32[64,1408]{1,0:T(8,128)S(1)}, f32[64,1408]{1,0:T(8,128)}, u32[]{:S(2)}) copy-start(f32[64,1408]{1,0:T(8,128)} %reduce-scatter.20.cloned.1.call-done) | copy-start | bytes 1081348
  1951.7 78.1 %copy-start.25 = (f32[64,1408]{1,0:T(8,128)S(1)}, f32[64,1408]{1,0:T(8,128)}, u32[]{:S(2)}) copy-start(f32[64,1408]{1,0:T(8,128)} %param.38) | copy-start | bytes 1081348
  (56 other events, 352.4 us)
Sparse Core Ops, SparseCore 0:
  10.3 135.9 all-gather.11
  148.0 47.5 all-gather.19
  197.8 142.8 all-gather.13
  342.8 162.4 all-gather.15
  507.3 162.4 all-gather.17
  671.9 45.6 all-gather.7
  719.8 143.9 all-gather.9
  906.7 165.2 reduce-scatter.13
  1074.7 69.5 reduce-scatter.9
  1146.7 164.6 reduce-scatter.19
  1313.9 184.5 reduce-scatter.17
  1500.9 184.2 reduce-scatter.15
  1687.8 186.9 reduce-scatter.11
  1877.5 71.1 reduce-scatter.7
where the time goes:
time: 2060 us
  waiting for transfers between devices  1690 us (82%)
  matrix products  118 us (6%)
  local copies, waits for them, and re-layouts  112 us (5%)
  blocking collectives  65.4 us (3%)
  other arithmetic  49.1 us (2%)
  between operations  20.8 us (1%)
    reduce_scatter x1, waiting for transfers between devices, body(): lax.psum_scatter(block_order(qkv_full, inverse, owners), 'dp', scatter_di...  188 us
    reduce_scatter x1, waiting for transfers between devices, body(): lax.psum_scatter(block_order(up_full, inverse, owners), 'dp', scatter_dim...  185 us
    reduce_scatter x1, waiting for transfers between devices, body(): lax.psum_scatter(block_order(gate_full, inverse, owners), 'dp', scatter_d...  185 us
    reduce_scatter x1, waiting for transfers between devices, body(): lax.psum_scatter(block_order(down_full, inverse, owners), 'dp', scatter_d...  165 us
    all_gather x1, waiting for transfers between devices, body(): lax.all_gather(down_weight.astype(jnp.bfloat16), 'dp', axis=0, tiled=True)  158 us
    all_gather x1, waiting for transfers between devices, body(): lax.all_gather(up_weight.astype(jnp.bfloat16), 'dp', axis=0, tiled=True)  158 us
    all_gather x1, waiting for transfers between devices, body(): lax.all_gather(gate_weight.astype(jnp.bfloat16), 'dp', axis=0, tiled=True)  141 us
    all_gather x1, waiting for transfers between devices, body(): lax.all_gather(qkv_weight.astype(jnp.bfloat16), 'dp', axis=0, tiled=True)  138 us
  transfers between devices with their start and end apart: 14, of which 14 were waited for; matrix products, arithmetic and copies ran while one was open for 10% of the time, Pallas kernels for 0%

commit v1 on v0

v1 whole, which is shorter than its diff:
```python
import math

import jax
import jax.numpy as jnp
from jax import lax
from jax.experimental import pallas as pl
from jax.experimental.pallas import tpu as pltpu
from jax.sharding import PartitionSpec as P

MESH = pl.DeviceIdType.MESH
BF = jnp.bfloat16
F32 = jnp.float32

HEAD_DIM = 64
ROT = 16
STEP = 5

NORM_EPSILON = 1e-05
BETA_ONE = 0.5
BETA_TWO = 0.5
ADAM_EPS = 1e-08
WEIGHT_DECAY = 0.01
RATE_LIST = (0.02, 0.1, 0.02, 0.02, 0.015)
NORM_RATE = 0.2
CLIP_LIMIT = 1.0
MASK_FILL = -1e30
PRECISE = lax.Precision.HIGHEST
ROWS_DIMS = (((0,), (0,)), ((), ()))
COLS_DIMS = (((1,), (1,)), ((), ()))

D = 2048
LEN = 512
ROWS = 64
TOK = 128
GROUP = 1024
HEADS = 4
CA = 2176
CB = 1024
CHUNKS = ((0, 0, 512), (0, 512, 512), (0, 1024, 512), (0, 1536, 640), (1, 0, 512), (1, 512, 512))


def place():
    dp = lax.axis_index("dp")
    mp = lax.axis_index("mp")
    return (mp // 2) * 2 + dp // 16, dp % 4, (dp // 4) % 4, mp % 2


def device(x, y, z, c):
    return ((x % 2) * 16 + z * 4 + y, (x // 2) * 2 + c)


def near(me, name):
    x, y, z, c = me
    return {
        "y+": lambda: device(x, (y + 1) % 4, z, c),
        "y-": lambda: device(x, (y + 3) % 4, z, c),
        "z+": lambda: device(x, y, (z + 1) % 4, c),
        "z-": lambda: device(x, y, (z + 3) % 4, c),
        "x+": lambda: device((x + 1) % 4, y, z, c),
        "x-": lambda: device((x + 3) % 4, y, z, c),
        "c": lambda: device(x, y, z, 1 - c),
        "p": lambda: device((x // 2) * 2 + 1 - x % 2, y, z, c),
    }[name]()


NEIGHBOURS = ("y+", "y-", "z+", "z-", "x+", "x-", "c")


def greet(me):
    barrier = pltpu.get_barrier_semaphore()
    for name in NEIGHBOURS:
        pl.semaphore_signal(barrier, inc=1, device_id=near(me, name), device_id_type=MESH)
    pl.semaphore_wait(barrier, len(NEIGHBOURS))


class Wires:
    def __init__(self, me, send, recv):
        self.me, self.send, self.recv = me, send, recv
        self.count = 0
        self.open = []

    def push(self, src, dst, name, at=None):
        if at is None:
            at = self.count
            self.count += 1
        copy = pltpu.make_async_remote_copy(
            src, dst, self.send.at[at], self.recv.at[at], device_id=near(self.me, name), device_id_type=MESH
        )
        copy.start()
        self.open.append(copy)
        return copy

    def take(self, number):
        at = self.count
        self.count += number
        return at

    def close(self):
        for copy in self.open:
            copy.wait_send()


def gather_kernel(own_a, own_b, tok, doc, wall_a, wall_b, toks, docs, send, recv, keep):
    me = x, y, z, c = place()
    xlo, xhi = x % 2, x // 2
    wires = Wires(me, send, recv)
    pairs = ((own_a, wall_a), (own_b, wall_b))
    locals_ = []

    def local(src, dst):
        copy = pltpu.make_async_copy(src, dst, keep.at[len(locals_)])
        copy.start()
        locals_.append(copy)

    greet(me)
    four = ("y+", "y-", "z+", "z-")
    first = wires.take(16)

    def own_at(i, half, d):
        return first + i * 8 + half * 4 + d

    for i, (own, wall) in enumerate(pairs):
        for d, name in enumerate(four):
            wires.push(own.at[xlo], wall.at[xlo, z, y], name, own_at(i, xlo, d))
    swaps = [wires.push(own.at[1 - xlo], wall.at[xlo, z, y], "p") for own, wall in pairs]
    doc_swap = wires.push(doc, docs.at[xlo], "p")
    local(doc, docs.at[xlo])
    for own, wall in pairs:
        local(own.at[xlo], wall.at[xlo, z, y])
    tok_x = {}
    tok_c = []
    for k in range(2):
        for name in ("x+", "x-"):
            tok_x[k, name] = wires.push(tok.at[k], toks.at[k, xlo, xhi, c], name)
        tok_c.append(wires.push(tok.at[k], toks.at[k, xlo, xhi, c], "c"))
        local(tok.at[k], toks.at[k, xlo, xhi, c])
    for i, (own, wall) in enumerate(pairs):
        swaps[i].wait_recv()
        for d, name in enumerate(four):
            mine = wall.at[1 - xlo, z, y]
            wires.push(mine, mine, name, own_at(i, 1 - xlo, d))

    axes = (("y+", "y-", "z+", "z-"), ("z+", "z-", "y+", "y-"))

    def block(wall, half, a, b):
        return wall.at[0, b, a] if half == 0 else wall.at[1, a, b]

    def spots(half):
        return (y, z) if half == 0 else (z, y)

    def wait_own(i, half, name):
        wall = pairs[i][1]
        mine = wall.at[half, z, y]
        at = own_at(i, half, four.index(name))
        pltpu.make_async_remote_copy(
            mine, mine, send.at[at], recv.at[at], device_id=near(me, name), device_id_type=MESH
        ).wait_recv()

    lo, hi = pl.ds(0, ROWS // 2), pl.ds(ROWS // 2, ROWS // 2)
    forwards, seconds = {}, {}
    for i, (own, wall) in enumerate(pairs):
        for half in range(2):
            a, b = spots(half)
            f_up, f_down, s_up, s_down = axes[half]
            wait_own(i, half, f_up)
            got = block(wall, half, (a + 3) % 4, b)
            forwards[i, half, 0] = wires.push(got.at[lo], got.at[lo], f_up)
            wait_own(i, half, f_down)
            other = block(wall, half, (a + 1) % 4, b)
            forwards[i, half, 1] = wires.push(other.at[hi], other.at[hi], f_down)
            for j, item in ((1, got), (2, other)):
                seconds[i, half, j, 0] = wires.push(item, item, s_up)
                seconds[i, half, j, 1] = wires.push(item, item, s_down)
    tok_f = {}
    for k in range(2):
        for n, name in enumerate(("x+", "x-")):
            tok_x[k, name].wait_recv()
            sx = (x + 3) % 4 if n == 0 else (x + 1) % 4
            got = toks.at[k, sx % 2, sx // 2, c]
            part = got.at[pl.ds(n * (TOK // 2), TOK // 2)]
            tok_f[k, n] = wires.push(part, part, name)
            tok_c.append(wires.push(got, got, "c"))
    for i, (own, wall) in enumerate(pairs):
        for half in range(2):
            a, b = spots(half)
            f_up, f_down, s_up, s_down = axes[half]
            forwards[i, half, 0].wait_recv()
            forwards[i, half, 1].wait_recv()
            item = block(wall, half, (a + 2) % 4, b)
            seconds[i, half, 3, 0] = wires.push(item, item, s_up)
            seconds[i, half, 3, 1] = wires.push(item, item, s_down)
    lasts = []
    for j, step in enumerate((0, 3, 1, 2)):
        for i, (own, wall) in enumerate(pairs):
            for half in range(2):
                a, b = spots(half)
                f_up, f_down, s_up, s_down = axes[half]
                spot = (a + step) % 4
                for n, name in ((0, s_up), (1, s_down)):
                    if j == 0:
                        wait_own(i, half, name)
                    else:
                        seconds[i, half, j, n].wait_recv()
                    got = block(wall, half, spot, (b + 3) % 4 if n == 0 else (b + 1) % 4)
                    part = got.at[lo if n == 0 else hi]
                    lasts.append(wires.push(part, part, name))
        if j == 1:
            for k in range(2):
                tok_f[k, 0].wait_recv()
                tok_f[k, 1].wait_recv()
                sx = (x + 2) % 4
                got = toks.at[k, sx % 2, sx // 2, c]
                tok_c.append(wires.push(got, got, "c"))
    for copy in lasts:
        copy.wait_recv()
    for copy in tok_c:
        copy.wait_recv()
    doc_swap.wait_recv()
    wires.close()
    for copy in locals_:
        copy.wait()


def gather_all(own_a, own_b, tok, doc):
    any_ = pl.BlockSpec(memory_space=pl.ANY)
    return pl.pallas_call(
        gather_kernel,
        out_shape=(
            jax.ShapeDtypeStruct((2, 4, 4, ROWS, CA), BF),
            jax.ShapeDtypeStruct((2, 4, 4, ROWS, CB), BF),
            jax.ShapeDtypeStruct((2, 2, 2, 2, TOK, D), BF),
            jax.ShapeDtypeStruct((2, 8, 128), F32),
        ),
        in_specs=[any_] * 4,
        out_specs=(any_,) * 4,
        scratch_shapes=[
            pltpu.SemaphoreType.DMA((160,)),
            pltpu.SemaphoreType.DMA((160,)),
            pltpu.SemaphoreType.DMA((8,)),
        ],
        compiler_params=pltpu.CompilerParams(collective_id=0, has_side_effects=True),
    )(own_a, own_b, tok, doc)


def add_rows(dst, src, rows, cols):
    def step(g, carry):
        at = pl.ds(pl.multiple_of(g * 16, 16), 16)
        dst[at, cols] = (dst[at, cols].astype(F32) + src[at, cols].astype(F32)).astype(dst.dtype)
        return carry

    lax.fori_loop(0, rows // 16, step, 0)


def scatter_kernel(
    part_a, part_b, branch, grad_a, grad_b, tok_out,
    o1_a, o1_b, o3_a, o3_b, r1_a, r1_b, r2_a, r2_b, t1_a, t1_b, t2_a, t2_b, sum_a, sum_b,
    own, core, x1, x2, send, recv, keep,
):
    me = x, y, z, c = place()
    xlo = x % 2
    wires = Wires(me, send, recv)
    parts, grads = (part_a, part_b), (grad_a, grad_b)
    o1, o3, r1, r2 = (o1_a, o1_b), (o3_a, o3_b), (r1_a, r1_b), (r2_a, r2_b)
    t1, t2, sums = (t1_a, t1_b), (t2_a, t2_b), (sum_a, sum_b)
    kept = []
    late = []

    def local(src, dst):
        copy = pltpu.make_async_copy(src, dst, keep.at[len(kept)])
        copy.start()
        kept.append(copy)
        return copy

    greet(me)
    axes = (("z+", "z-", "y+", "y-"), ("y+", "y-", "z+", "z-"))

    def spots(half):
        return (z, y) if half == 0 else (y, z)

    def piece(half, chunk, spot, start, size):
        i, c0, cn = chunk
        cols = pl.ds(c0, cn)
        if half == 0:
            return parts[i].at[0, spot, pl.ds(start, size), :, cols]
        return parts[i].at[1, pl.ds(start, size), spot, :, cols]

    state = {}

    def tokens_start():
        for k in range(2):
            state["c", k] = wires.push(branch.at[k, :, :, 1 - c], core.at[k], "c")
            state["l", k] = local(branch.at[k, :, :, c], own.at[k])

    def stage0(n, half):
        chunk = i, c0, cn = CHUNKS[n]
        p, q = spots(half)
        up, down = axes[half][:2]
        cols = pl.ds(c0, cn)
        state["a", n, half, 0] = wires.push(
            piece(half, chunk, (p + 2) % 4, 0, 2), r1[i].at[half, 0, :, :, cols], up
        )
        state["a", n, half, 1] = wires.push(
            piece(half, chunk, (p + 2) % 4, 2, 2), r1[i].at[half, 1, :, :, cols], down
        )
        state["o", n, half, 0] = local(piece(half, chunk, (p + 1) % 4, 0, 2), o1[i].at[half, 0, :, :, cols])
        state["o", n, half, 1] = local(piece(half, chunk, (p + 3) % 4, 2, 2), o1[i].at[half, 1, :, :, cols])
        state["b", n, half, 0] = wires.push(
            piece(half, chunk, (p + 1) % 4, 2, 2), r2[i].at[half, 0, pl.ds(2, 2), :, cols], up
        )
        state["b", n, half, 1] = wires.push(
            piece(half, chunk, (p + 3) % 4, 0, 2), r2[i].at[half, 1, pl.ds(0, 2), :, cols], down
        )
        state["o3", n, half] = local(piece(half, chunk, p, 0, 4), o3[i].at[half, :, :, cols])

    def stage1(n, half):
        i, c0, cn = CHUNKS[n]
        cols = pl.ds(c0, cn)
        for d in range(2):
            state["a", n, half, d].wait_recv()
            state["o", n, half, d].wait()
            for m in range(2):
                add_rows(o1[i].at[half, d, m], r1[i].at[half, d, m], ROWS, cols)
            state["s", n, half, d] = wires.push(
                o1[i].at[half, d, :, :, cols], r2[i].at[half, d, pl.ds(2 * d, 2), :, cols], axes[half][d]
            )

    def stage2(n, half):
        i, c0, cn = CHUNKS[n]
        cols = pl.ds(c0, cn)
        p, q = spots(half)
        up, down = axes[half][2:]
        for d in range(2):
            state["b", n, half, d].wait_recv()
            state["s", n, half, d].wait_recv()
        state["o3", n, half].wait()

        def step(g, carry):
            at = pl.ds(pl.multiple_of((g % 4) * 16, 16), 16)
            m = g // 4
            total = (
                o3[i][half, m, at, cols].astype(F32)
                + r2[i][half, 0, m, at, cols].astype(F32)
                + r2[i][half, 1, m, at, cols].astype(F32)
            )
            o3[i][half, m, at, cols] = total.astype(BF)
            return carry

        lax.fori_loop(0, 16, step, 0)
        far = o3[i].at[half, (q + 2) % 4]
        lo, hi = pl.ds(0, ROWS // 2), pl.ds(ROWS // 2, ROWS // 2)
        state["t", n, half, 0] = wires.push(far.at[lo, cols], t1[i].at[half, 0, :, cols], up)
        state["t", n, half, 1] = wires.push(far.at[hi, cols], t1[i].at[half, 1, :, cols], down)
        state["u", n, half, 0] = wires.push(
            o3[i].at[half, (q + 1) % 4, hi, cols], t2[i].at[half, 0, hi, cols], up
        )
        state["u", n, half, 1] = wires.push(
            o3[i].at[half, (q + 3) % 4, lo, cols], t2[i].at[half, 1, lo, cols], down
        )

    def stage3(n, half):
        i, c0, cn = CHUNKS[n]
        cols = pl.ds(c0, cn)
        p, q = spots(half)
        for d in range(2):
            state["t", n, half, d].wait_recv()
            rows = pl.ds(d * (ROWS // 2), ROWS // 2)
            spot = (q + 1) % 4 if d == 0 else (q + 3) % 4
            mine = o3[i].at[half, spot, rows]
            add_rows(mine, t1[i].at[half, d], ROWS // 2, cols)
            state["v", n, half, d] = wires.push(
                mine.at[:, cols], t2[i].at[half, d, rows, cols], axes[half][2 + d]
            )

    def stage4(n, half):
        i, c0, cn = CHUNKS[n]
        cols = pl.ds(c0, cn)
        p, q = spots(half)
        for d in range(2):
            state["u", n, half, d].wait_recv()
            state["v", n, half, d].wait_recv()

        def step(g, carry):
            at = pl.ds(pl.multiple_of(g * 16, 16), 16)
            total = (
                o3[i][half, q, at, cols].astype(F32)
                + t2[i][half, 0, at, cols].astype(F32)
                + t2[i][half, 1, at, cols].astype(F32)
            )
            sums[i][half, at, cols] = total
            return carry

        lax.fori_loop(0, ROWS // 16, step, 0)

    def stage5(n):
        i, c0, cn = CHUNKS[n]
        cols = pl.ds(c0, cn)
        state["g", n] = wires.push(sums[i].at[1 - xlo, :, cols], grads[i].at[xlo, :, cols], "p")
        late.append(local(sums[i].at[xlo, :, cols], grads[i].at[xlo, :, cols]))

    half_tok = TOK // 2

    def tokens1(k):
        state["c", k].wait_recv()
        state["l", k].wait()

        def step(g, carry):
            at = pl.ds(pl.multiple_of((g % 8) * 16, 16), 16)
            s = g // 8
            own[k, s // 2, s % 2, at, :] = (
                own[k, s // 2, s % 2, at, :].astype(F32) + core[k, s // 2, s % 2, at, :].astype(F32)
            ).astype(BF)
            return carry

        lax.fori_loop(0, 32, step, 0)

        def spot(s, d, far):
            rows = pl.ds((d if far else 1 - d) * half_tok, half_tok)
            return own.at[k, s % 2, s // 2, rows]

        for d, name in enumerate(("x+", "x-")):
            state["x1", k, d] = wires.push(spot((x + 2) % 4, d, True), x1.at[k, d], name)
        for d, name in enumerate(("x+", "x-")):
            to = (x + 1) % 4 if d == 0 else (x + 3) % 4
            rows = pl.ds((1 - d) * half_tok, half_tok)
            state["x2", k, d] = wires.push(spot(to, d, False), x2.at[k, d, rows], name)

    def tokens2(k):
        for d, name in enumerate(("x+", "x-")):
            state["x1", k, d].wait_recv()
            to = (x + 1) % 4 if d == 0 else (x + 3) % 4
            rows = pl.ds(d * half_tok, half_tok)
            mine = own.at[k, to % 2, to // 2, rows]
            add_rows(mine, x1.at[k, d], half_tok, pl.ds(0, D))
            state["x3", k, d] = wires.push(mine, x2.at[k, d, rows], name)

    def tokens3(k):
        for d in range(2):
            state["x2", k, d].wait_recv()
            state["x3", k, d].wait_recv()

        def step(g, carry):
            at = pl.ds(pl.multiple_of(g * 16, 16), 16)
            tok_out[k, at, :] = (
                own[k, xlo, x // 2, at, :].astype(F32)
                + x2[k, 0, at, :].astype(F32)
                + x2[k, 1, at, :].astype(F32)
            )
            return carry

        lax.fori_loop(0, TOK // 16, step, 0)

    tokens_start()
    stages = (stage1, stage2, stage3, stage4)
    total = len(CHUNKS)
    for t in range(-1, total + 5):
        if t + 1 < total:
            for half in range(2):
                stage0(t + 1, half)
        for s, stage in enumerate(stages):
            n = t - s
            if 0 <= n < total:
                for half in range(2):
                    stage(n, half)
        if 0 <= t - 3 < total:
            stage5(t - 3)
        if t in (0, 1):
            tokens1(t)
        if t in (2, 3):
            tokens2(t - 2)
        if t in (4, 5):
            tokens3(t - 4)
    for n in range(total):
        state["g", n].wait_recv()
    wires.close()
    for copy in late:
        copy.wait()


def scatter_all(part_a, part_b, branch):
    any_ = pl.BlockSpec(memory_space=pl.ANY)
    vmem = pl.BlockSpec(memory_space=pltpu.VMEM)

    def both(*shape, dtype=BF):
        return [pltpu.VMEM(shape + (CA,), dtype), pltpu.VMEM(shape + (CB,), dtype)]

    return pl.pallas_call(
        scatter_kernel,
        out_shape=(
            jax.ShapeDtypeStruct((2, ROWS, CA), F32),
            jax.ShapeDtypeStruct((2, ROWS, CB), F32),
            jax.ShapeDtypeStruct((2, TOK, D), F32),
        ),
        in_specs=[any_] * 3,
        out_specs=(any_, any_, vmem),
        scratch_shapes=[
            *both(2, 2, 2, ROWS),
            *both(2, 4, ROWS),
            *both(2, 2, 2, ROWS),
            *both(2, 2, 4, ROWS),
            *both(2, 2, ROWS // 2),
            *both(2, 2, ROWS),
            *both(2, ROWS, dtype=F32),
            pltpu.VMEM((2, 2, 2, TOK, D), BF),
            pltpu.VMEM((2, 2, 2, TOK, D), BF),
            pltpu.VMEM((2, 2, TOK // 2, D), BF),
            pltpu.VMEM((2, 2, TOK, D), BF),
            pltpu.SemaphoreType.DMA((192,)),
            pltpu.SemaphoreType.DMA((192,)),
            pltpu.SemaphoreType.DMA((64,)),
        ],
        compiler_params=pltpu.CompilerParams(
            collective_id=1, has_side_effects=True, vmem_limit_bytes=56 * 2**20
        ),
    )(part_a, part_b, branch)


def total_kernel(item, out, first, second, send1, recv1, send2, recv2):
    x, y, z, c = place()
    here, there = z * 4 + y, x * 2 + c

    def plane(k):
        at = (here + k) % 16
        return device(x, at % 4, at // 4, c)

    def line(k):
        at = (there + k) % 8
        return device(at // 2, y, z, at % 2)

    barrier = pltpu.get_barrier_semaphore()
    for k in range(1, 16):
        pl.semaphore_signal(barrier, inc=1, device_id=plane(k), device_id_type=MESH)
    for k in range(1, 8):
        pl.semaphore_signal(barrier, inc=1, device_id=line(k), device_id_type=MESH)
    first[here] = item[...]
    pl.semaphore_wait(barrier, 22)
    copies = []
    for k in range(1, 16):
        copies.append(
            pltpu.make_async_remote_copy(
                first.at[here], first.at[here], send1.at[k], recv1.at[k], device_id=plane(k), device_id_type=MESH
            )
        )
        copies[-1].start()
    for copy in copies:
        copy.wait_recv()
    total = first[0]
    for k in range(1, 16):
        total = total + first[k]
    second[there] = total
    others = []
    for k in range(1, 8):
        others.append(
            pltpu.make_async_remote_copy(
                second.at[there], second.at[there], send2.at[k], recv2.at[k], device_id=line(k), device_id_type=MESH
            )
        )
        others[-1].start()
    for copy in others:
        copy.wait_recv()
    total = second[0]
    for k in range(1, 8):
        total = total + second[k]
    out[...] = total
    for copy in copies + others:
        copy.wait_send()


def total_all(item):
    vmem = pl.BlockSpec(memory_space=pltpu.VMEM)
    return pl.pallas_call(
        total_kernel,
        out_shape=jax.ShapeDtypeStruct(item.shape, F32),
        in_specs=[vmem],
        out_specs=vmem,
        scratch_shapes=[
            pltpu.VMEM((16,) + item.shape, F32),
            pltpu.VMEM((8,) + item.shape, F32),
            pltpu.SemaphoreType.DMA((16,)),
            pltpu.SemaphoreType.DMA((16,)),
            pltpu.SemaphoreType.DMA((8,)),
            pltpu.SemaphoreType.DMA((8,)),
        ],
        compiler_params=pltpu.CompilerParams(collective_id=2, has_side_effects=True),
    )(item)


def doc_layout(lengths, total):
    ends = jnp.cumsum(lengths)
    index = jnp.arange(total, dtype=jnp.int32)
    passed = (index[:, None] >= ends[None, :]).astype(jnp.int32)
    doc_ids = jnp.sum(passed, 1)
    starts = jnp.sum(passed * lengths[None, :], 1)
    return (doc_ids, index - starts, index)


def turn_angles(positions):
    half = ROT // 2
    freq = 10000.0 ** (-2.0 * jnp.arange(half, dtype=F32) / ROT)
    angle = positions.astype(F32)[..., None] * freq
    return (jnp.cos(angle)[:, :, None, :], jnp.sin(angle)[:, :, None, :])


def rotate(field, cosine, sine):
    half = ROT // 2
    lead_half = field[..., :half]
    tail_half = field[..., half:ROT]
    return jnp.concatenate(
        [
            lead_half * cosine - tail_half * sine,
            tail_half * cosine + lead_half * sine,
            field[..., ROT:],
        ],
        -1,
    )


def soap_update(weight, grad, first, second, basis, rate):
    rows, cols = grad.shape
    blocks = basis.shape[0]
    turned = jnp.einsum(
        "rbi,bij->rbj", grad.reshape(rows, blocks, -1), basis, precision=PRECISE
    ).reshape(rows, cols)
    first_new = BETA_ONE * first + (1.0 - BETA_ONE) * turned
    second_new = BETA_TWO * second + (1.0 - BETA_TWO) * turned * turned
    ratio = (
        first_new
        / (1.0 - BETA_ONE**STEP)
        / (jnp.sqrt(second_new / (1.0 - BETA_TWO**STEP)) + ADAM_EPS)
    )
    back = jnp.einsum(
        "rbj,bij->rbi", ratio.reshape(rows, blocks, -1), basis, precision=PRECISE
    ).reshape(rows, cols)
    return (first_new, second_new, weight - rate * (back + WEIGHT_DECAY * weight))


def adam_plain(param, grad, first, second, rate):
    first_new = BETA_ONE * first + (1.0 - BETA_ONE) * grad
    second_new = BETA_TWO * second + (1.0 - BETA_TWO) * grad * grad
    ratio = (
        first_new
        / (1.0 - BETA_ONE**STEP)
        / (jnp.sqrt(second_new / (1.0 - BETA_TWO**STEP)) + ADAM_EPS)
    )
    return (first_new, second_new, param - rate * ratio)


def split_columns(qkv, out, gate, up, down):
    zeros = jnp.zeros((ROWS, 64), qkv.dtype)
    a = jnp.stack(
        [
            jnp.concatenate(
                [qkv[:, :768], gate[:, :640], up[:, :640], gate[:, 640:704], up[:, 640:704]], 1
            ),
            jnp.concatenate(
                [qkv[:, 768:], gate[:, 768:], up[:, 768:], gate[:, 704:768], up[:, 704:768]], 1
            ),
        ]
    )
    b = jnp.stack(
        [
            jnp.concatenate([out[:, :256], down[:, :640], down[:, 640:704], zeros], 1),
            jnp.concatenate([out[:, 256:], down[:, 768:], down[:, 704:768], zeros], 1),
        ]
    )
    return a, b


def join_columns(a, b):
    def joined(item, start, rest):
        return jnp.concatenate(
            [
                item[0, :, start : start + 640],
                item[0, :, rest : rest + 64],
                item[1, :, rest : rest + 64],
                item[1, :, start : start + 640],
            ],
            1,
        )

    qkv = jnp.concatenate([a[0, :, :768], a[1, :, :768]], 1)
    out = jnp.concatenate([b[0, :, :256], b[1, :, :256]], 1)
    return (qkv, out, joined(a, 768, 2048), joined(a, 1408, 2112), joined(b, 256, 896))


def attention(qkv_pre, d_attn_of, lengths):
    docs, positions, index = jax.vmap(lambda one: doc_layout(one, LEN))(lengths)
    cosine, sine = turn_angles(positions)
    scale = 1.0 / math.sqrt(HEAD_DIM)
    queries = (rotate(qkv_pre[:, :, :, 0], cosine, sine) * scale).astype(BF)
    keys = rotate(qkv_pre[:, :, :, 1], cosine, sine).astype(BF)
    values = qkv_pre[:, :, :, 2].astype(BF)
    allowed = (docs[:, :, None] == docs[:, None, :]) & (index[:, :, None] >= index[:, None, :])
    allowed = allowed[:, None]
    scores = jnp.einsum("sqhd,skhd->shqk", queries, keys, preferred_element_type=F32)
    scores = jnp.where(allowed, scores, MASK_FILL)
    peak = jnp.max(scores, -1, keepdims=True)
    expo = jnp.exp(scores - peak)
    probs = expo / jnp.sum(expo, -1, keepdims=True)
    probs_low = probs.astype(BF)
    attn = jnp.einsum("shqk,skhd->sqhd", probs_low, values, preferred_element_type=F32)
    attn = attn.reshape(GROUP, HEADS * HEAD_DIM).astype(BF)
    d_attn = d_attn_of.reshape(2, LEN, HEADS, HEAD_DIM)
    d_prob = jnp.einsum("sqhd,skhd->shqk", d_attn, values, preferred_element_type=F32)
    delta = jnp.sum(probs * d_prob, -1, keepdims=True)
    d_score = (probs * (d_prob - delta)).astype(BF)
    d_query = jnp.einsum("shqk,skhd->sqhd", d_score, keys, preferred_element_type=F32) * scale
    d_key = jnp.einsum("shqk,sqhd->skhd", d_score, queries, preferred_element_type=F32)
    d_value = jnp.einsum("shqk,sqhd->skhd", probs_low, d_attn, preferred_element_type=F32)
    d_qkv = jnp.stack([rotate(d_query, cosine, -sine), rotate(d_key, cosine, -sine), d_value], 3)
    return attn, d_qkv.reshape(GROUP, HEADS * 3 * HEAD_DIM).astype(BF)


def body(
    tokens,
    cotangent,
    doc_lengths,
    row_owner,
    norm_params,
    norm_moment1,
    norm_moment2,
    qkv_weight,
    out_weight,
    gate_weight,
    up_weight,
    down_weight,
    qkv_moment1,
    out_moment1,
    gate_moment1,
    up_moment1,
    down_moment1,
    qkv_moment2,
    out_moment2,
    gate_moment2,
    up_moment2,
    down_moment2,
    qkv_basis,
    out_basis,
    gate_basis,
    up_basis,
    down_basis,
):
    stored_at = (row_owner[:, None] * ROWS + jnp.arange(ROWS, dtype=jnp.int32)[None, :]).reshape(D)
    turn = (stored_at[:, None] == jnp.arange(D, dtype=jnp.int32)[None, :]).astype(BF)
    pair = jnp.dot(jnp.concatenate([tokens, cotangent], 0), turn, preferred_element_type=F32)
    inputs = pair[:TOK]
    grad_in = pair[TOK:]
    inverse = jnp.argsort(row_owner)
    params_stored = norm_params.reshape(2, 32, ROWS)[:, inverse].reshape(2, D)
    norm_gain = params_stored[0]
    norm_shift = params_stored[1]
    row_mean = jnp.mean(inputs, -1, keepdims=True)
    centered_input = inputs - row_mean
    row_variance = jnp.mean(centered_input * centered_input, -1, keepdims=True)
    inverse_deviation = lax.rsqrt(row_variance + NORM_EPSILON)
    standardized_input = centered_input * inverse_deviation
    normed_output = (standardized_input * norm_gain + norm_shift).astype(BF)

    own_a, own_b = split_columns(
        *[item.astype(BF) for item in (qkv_weight, out_weight, gate_weight, up_weight, down_weight)]
    )
    doc_item = jnp.zeros((8, 128), F32).at[0, :4].set(doc_lengths[0].astype(F32))
    wall_a, wall_b, toks, docs = gather_all(
        own_a, own_b, jnp.stack([normed_output, grad_in.astype(BF)]), doc_item
    )
    wall_a = wall_a.reshape(D, CA)
    wall_b = wall_b.reshape(D, CB)
    normed_all = toks[0].reshape(GROUP, D)
    grad_all = toks[1].reshape(GROUP, D)
    lengths = docs[:, 0, :4].astype(jnp.int32)

    pre_a = jnp.dot(normed_all, wall_a, preferred_element_type=F32)
    pre_b = jnp.dot(grad_all, wall_b, preferred_element_type=F32)
    attn, d_qkv = attention(
        pre_a[:, :768].reshape(2, LEN, HEADS, 3, HEAD_DIM), pre_b[:, :256].astype(BF), lengths
    )

    def units(gate, up, d_hidden):
        sigma = jax.nn.sigmoid(gate)
        hidden = (gate * sigma * up).astype(BF)
        d_gate = (d_hidden * up * sigma * (1.0 + gate * (1.0 - sigma))).astype(BF)
        d_up = (d_hidden * gate * sigma).astype(BF)
        return hidden, d_gate, d_up

    hidden0, d_gate0, d_up0 = units(pre_a[:, 768:1408], pre_a[:, 1408:2048], pre_b[:, 256:896])
    hidden1, d_gate1, d_up1 = units(pre_a[:, 2048:2112], pre_a[:, 2112:2176], pre_b[:, 896:960])
    made = jnp.concatenate([attn, hidden0, hidden1, jnp.zeros((GROUP, 64), BF)], 1)
    back = jnp.concatenate([d_qkv, d_gate0, d_up0, d_gate1, d_up1], 1)
    branch = lax.dot_general(made, wall_b, COLS_DIMS, preferred_element_type=F32).astype(BF)
    d_normed = lax.dot_general(back, wall_a, COLS_DIMS, preferred_element_type=F32).astype(BF)
    part_a = lax.dot_general(normed_all, back, ROWS_DIMS, preferred_element_type=F32).astype(BF)
    part_b = lax.dot_general(grad_all, made, ROWS_DIMS, preferred_element_type=F32).astype(BF)
    grad_a, grad_b, tok_sums = scatter_all(
        part_a.reshape(2, 4, 4, ROWS, CA),
        part_b.reshape(2, 4, 4, ROWS, CB),
        jnp.stack([branch, d_normed]).reshape(2, 2, 2, 2, TOK, D),
    )

    out = (inputs + tok_sums[0]).astype(BF)
    normed_cotangent = tok_sums[1]
    standardized_cotangent = normed_cotangent * norm_gain
    input_grad = (
        grad_in
        + inverse_deviation
        * (
            standardized_cotangent
            - jnp.mean(standardized_cotangent, -1, keepdims=True)
            - standardized_input
            * jnp.mean(standardized_cotangent * standardized_input, -1, keepdims=True)
        )
    ).astype(BF)
    pair_out = lax.dot_general(
        jnp.concatenate([out, input_grad], 0), turn, COLS_DIMS, preferred_element_type=F32
    ).astype(BF)

    norm_partial = jnp.stack(
        [jnp.sum(normed_cotangent * standardized_input, 0), jnp.sum(normed_cotangent, 0)]
    )
    squares = jnp.sum((grad_a * grad_a).reshape(-1, 128), 0) + jnp.sum((grad_b * grad_b).reshape(-1, 128), 0)
    item = jnp.concatenate(
        [norm_partial.reshape(8, 512), jnp.zeros((8, 128), F32).at[0].set(squares)], 1
    )
    totals = total_all(item)
    norm_raw = totals[:, :512].reshape(2, 32, ROWS)[:, row_owner].reshape(2, D)
    grad_norm = jnp.sqrt(jnp.sum(totals[:, 512:]) + jnp.sum(norm_raw * norm_raw))
    clip = jnp.minimum(1.0, CLIP_LIMIT / grad_norm)
    norm_grads = clip * norm_raw
    norm_first, norm_second, norm_new = adam_plain(
        norm_params, norm_grads, norm_moment1, norm_moment2, NORM_RATE
    )
    masters = (qkv_weight, out_weight, gate_weight, up_weight, down_weight)
    firsts = (qkv_moment1, out_moment1, gate_moment1, up_moment1, down_moment1)
    seconds = (qkv_moment2, out_moment2, gate_moment2, up_moment2, down_moment2)
    bases = (qkv_basis, out_basis, gate_basis, up_basis, down_basis)
    clipped = [clip * grad for grad in join_columns(grad_a, grad_b)]
    updates = [
        soap_update(masters[i], clipped[i], firsts[i], seconds[i], bases[i], RATE_LIST[i])
        for i in range(5)
    ]
    return (
        pair_out[:TOK],
        pair_out[TOK:],
        grad_norm,
        norm_grads,
        norm_first,
        norm_second,
        norm_new,
        *clipped,
        *[item[0] for item in updates],
        *[item[1] for item in updates],
        *[item[2] for item in updates],
    )


def solution(mesh):
    tok, weight, whole = P(("dp", "mp"), None), P("dp", "mp"), P()
    in_specs = (tok, tok, P("dp", None)) + (whole,) * 4 + (weight,) * 15 + (P("mp", None, None),) * 5
    out_specs = (tok, tok) + (whole,) * 5 + (weight,) * 20
    return jax.shard_map(body, mesh=mesh, in_specs=in_specs, out_specs=out_specs, check_vma=False)
```

time: 2060 us -> 428 us (0.21)
  waiting for transfers between devices: 1690 us -> 0 us
  Pallas kernels: 0 us -> 176 us
  blocking collectives: 65.4 us -> 0 us
  local copies, waits for them, and re-layouts: 112 us -> 74.6 us
    reduce_scatter x7 -> x0, waiting for transfers between devices: 883 us -> none  [the longest x1 188 us: body(): lax.psum_scatter(block_order(qkv_full, inverse, owners), 'dp', scatter_di...]
    all_gather x7 -> x0, waiting for transfers between devices: 806 us -> none  [the longest x1 158 us: body(): lax.all_gather(down_weight.astype(jnp.bfloat16), 'dp', axis=0, tiled=True)]
    pallas_call x0 -> x3, Pallas kernels: none -> 176 us  [the longest x1 82.3 us: scatter_all(): pl.pallas_call(scatter_kernel, out_shape=(jax.ShapeDtypeStruct((2, ROWS,...]
    gather x10 -> x2, local copies, waits for them, and re-layouts: 72.8 us -> 1.34 us  [the longest x1 0.73 us: body(): norm_raw = totals[:, :512].reshape(2, 32, ROWS)[:, row_owner].reshape(2, D)]
    psum x1 -> x0, blocking collectives: 65.4 us -> none  [body(): square_total = lax.psum(squares, ('dp', 'mp'))]
    slice x3 -> x21, local copies, waits for them, and re-layouts: 0.91 us -> 23.9 us  [the longest x2 7.29 us: body(): pre_a[:, :768].reshape(2, LEN, HEADS, 3, HEAD_DIM)]
    dot_general x21 -> x13, matrix products: 105 us -> 86.2 us  [the longest x1 15.5 us: body(): lax.dot_general(back, wall_a, COLS_DIMS, preferred_element_type=F32)]
  transfers between devices with their start and end apart: 14 -> 0, of which waited for: 14 -> 0; matrix products, arithmetic and copies ran while one was open for 10% -> 0% of each run, Pallas kernels for 0% -> 0%
where the time goes in v1:
time: 428 us; the launch traced here: 421 us
  Pallas kernels  176 us (41%)
  matrix products  108 us (25%)
  local copies, waits for them, and re-layouts  74.6 us (17%)
  other arithmetic  57.6 us (13%)
  between operations  4.46 us (1%)
    pallas_call x1, Pallas kernels, scatter_all(): pl.pallas_call(scatter_kernel, out_shape=(jax.ShapeDtypeStruct((2, ROWS,...  82.3 us
    pallas_call x1, Pallas kernels, gather_all(): pl.pallas_call(gather_kernel, out_shape=(jax.ShapeDtypeStruct((2, 4, 4, R...  76.2 us
    pallas_call x1, Pallas kernels, total_all(): pl.pallas_call(total_kernel, out_shape=jax.ShapeDtypeStruct(item.shape, F...  17.8 us
    dot_general x1, matrix products, body(): lax.dot_general(back, wall_a, COLS_DIMS, preferred_element_type=F32)  15.5 us
    unnamed x145, local copies, waits for them, and re-layouts  15.4 us
    dot_general x1, matrix products, body(): lax.dot_general(normed_all, back, ROWS_DIMS, preferred_element_type=F32)  14.4 us
    dot_general x1, matrix products, body(): pre_a = jnp.dot(normed_all, wall_a, preferred_element_type=F32)  14.3 us
    dot_general x1, matrix products, body(): lax.dot_general(made, wall_b, COLS_DIMS, preferred_element_type=F32)  9.46 us

profile of v1, /device:TPU:1, one launch (start us, length us, event | category | flops | bytes accessed | tf_op | source)
XLA Modules:
  0.0 421.0 jit_solution(9733636463004022532)
XLA Ops:
  13.7 3.3 fusion.2
  19.6 76.2 %shard_map.466 = (bf16[2,4,4,64,2176]{4,3,2,1,0:T(8,128)(2,1)}, bf16[2,4,4,64,1024]{4,3,2,1,0:T(8,128)(2,1)}, bf16[2,2,2,2,128,2048]{5,4,3,2,1,0:T(8,128)(2,1)}, f32[2,8,128]{2,1,0:T(8,128)}) custom-call(bf16[2,64,2176]{2,1,0:T(8,128)(2,1)} %pad_maximum_fusion.3.own_a, bf16[2,64,1024]{2,1,0:T(8,128)(2,1)} %pad_maximum_fusion.5.own_b, ...), custom_call_target="tpu_custom_call" | custom-call | tf_op jit(solution)/shard_map/pallas_call | solution.py:226
  95.8 6.4 %fusion.109 = (bf16[1,2,2,2,128,2048]{5,4,3,2,1,0:T(8,128)(2,1)}, bf16[1,2,2,2,128,2048]{5,4,3,2,1,0:T(8,128)(2,1)}) fusion(bf16[2,2,2,2,128,2048]{5,4,3,2,1,0:T(8,128)(2,1)} %get-tuple-element.60), kind=kLoop, calls=%fused_computation.233 | loop fusion | bytes 16777216 | tf_op jit(solution)/shard_map/slice | solution.py:768
  105.2 7.6 %fusion.126 = f32[1024,1024]{0,1:T(8,128)S(1)} fusion(bf16[1024,2048]{1,0:T(8,128)(2,1)} %bitcast.270, bf16[2048,1024]{1,0:T(8,128)(2,1)} %bitcast.286), kind=kOutput, calls=%fused_computation.246 | convolution fusion | flops 4294967296 | bytes 12582912 | tf_op jit(solution)/shard_map/dot_general | solution.py:772
  115.6 2.4 reshape.307
  120.1 14.3 %fusion.125 = f32[1024,2176]{1,0:T(8,128)S(1)} fusion(bf16[1024,2048]{1,0:T(8,128)(2,1)} %bitcast.268, bf16[2048,2176]{1,0:T(8,128)(2,1)} %bitcast.284), kind=kOutput, calls=%fused_computation.245 | convolution fusion | flops 9126805504 | bytes 22020096 | tf_op jit(solution)/shard_map/dot_general | solution.py:771
  134.5 3.3 copy-done.7
  144.8 4.5 %multiply_convert_fusion.2 = (bf16[1024,640]{1,0:T(8,128)(2,1)}, bf16[1024,640]{1,0:T(8,128)(2,1)}, bf16[1024,640]{1,0:T(8,128)(2,1)}) fusion(f32[1024,640]{1,0:T(8,128)S(1)} %copy-done.5, f32[1024,2176]{1,0:T(8,128)} %copy-done.7), kind=kLoop, calls=%fused_computation.22 | loop fusion | flops 10485760 | bytes 11796480 | tf_op jit(solution)/shard_map/convert_element_type | solution.py:781
  149.3 3.8 slice.330
  153.0 3.5 copy.209
  156.6 5.7 %reshape.305 = f32[2,512,4,3,64]{1,0,4,3,2:T(2,128)} reshape(f32[1024,768]{0,1:T(8,128)} %copy.209) | data formatting | bytes 6291456 | tf_op jit(solution)/shard_map/reshape | solution.py:774
  163.4 2.4 slice.340
  172.6 7.9 %fusion.120 = (f32[2,4,512]{2,1,0:T(4,128)S(1)}, f32[2,4,512,512]{2,3,1,0:T(8,128)}) fusion(pred[2,512,512]{1,2,0:T(8,128)(4,1)} %fusion.15, bf16[2,512,4,48]{1,3,2,0:T(8,128)(2,1)} %slice.431, bf16[2,512,4,8]{1,3,2,0:T(8,128)(2,1)} %get-tuple-element.145, bf16[2,512,4,8]{1,3,2,0:T(8,128)(2,1)} %get-tuple-element.146, f32[2,512,4,48]{1,3,2,0:T(8,128)} %slice.338, ...), kind=kOutput, calls=%fused_computation.244 | convolution fusion | flops 277348864 | bytes 10502144 | tf_op jit(solution)/shard_map/sub | solution.py:697
  180.6 5.9 %fusion.26 = bf16[2,512,4,1,64]{1,4,2,0,3:T(8,128)(2,1)} fusion(bf16[2,512,4,64]{1,0,3,2:T(2,128)(2,1)} %reshape.307, f32[2,4,512,512]{2,3,1,0:T(8,128)} %get-tuple-element.157, f32[2,4,512]{2,1,0:T(4,128)S(1)} %get-tuple-element.156), kind=kOutput, calls=%fused_computation.40 | convolution fusion | flops 272891904 | bytes 9453568 | tf_op jit(solution)/shard_map/shqk,sqhd->skhd/dot_general | solution.py:708
  190.5 2.7 reshape.347
  193.3 9.5 %convolution_convert_fusion.2 = bf16[1024,2048]{1,0:T(8,128)(2,1)} fusion(bf16[2048,1024]{1,0:T(8,128)(2,1)} %bitcast.287, bf16[1024,64]{1,0:T(8,128)(2,1)} %copy.227, bf16[1024,640]{1,0:T(8,128)(2,1)} %get-tuple-element.94, bf16[1024,256]{1,0:T(8,128)(2,1)} %reshape.347, bf16[1024]{0:T(1024)(128)(2,1)} %copy-done.57), kind=kOutput, calls=%fused_computation.19 | convolution fusion | flops 4305453056 | bytes 10356736 | tf_op jit(solution)/shard_map/dot_general | solution.py:788
  202.8 6.8 %convolution_convert_fusion.3 = bf16[2048,1024]{1,0:T(8,128)(2,1)} fusion(bf16[1024,2048]{1,0:T(8,128)(2,1)S(1)} %bitcast.271, bf16[1024,64]{1,0:T(8,128)(2,1)S(1)} %copy-done.48, bf16[1024,640]{1,0:T(8,128)(2,1)S(1)} %copy-done.27, bf16[1024,256]{1,0:T(8,128)(2,1)S(1)} %copy-done.29, bf16[1024]{0:T(1024)(128)(2,1)S(1)} %copy-done.58), kind=kOutput, calls=%fused_computation.20 | convolution fusion | flops 4305453056 | bytes 10356736 | tf_op jit(solution)/shard_map/dot_general | solution.py:791
  211.3 2.4 multiply_convert_fusion
  221.0 15.5 %convolution_convert_fusion.1 = bf16[1024,2048]{1,0:T(8,128)(2,1)} fusion(bf16[1024,2176]{0,1:T(8,128)(2,1)S(1)} %fusion.80, bf16[2048,2176]{1,0:T(8,128)(2,1)} %bitcast.285), kind=kOutput, calls=%fused_computation.18 | convolution fusion | flops 9128902656 | bytes 17563648 | tf_op jit(solution)/shard_map/dot_general | solution.py:789
  236.5 7.8 %pad_maximum_fusion.branch = bf16[2,2,2,2,128,2048]{5,4,3,2,1,0:T(8,128)(2,1)} fusion(bf16[1,2,2,2,128,2048]{5,4,3,2,1,0:T(8,128)(2,1)} %bitcast.274, bf16[1,2,2,2,128,2048]{5,4,3,2,1,0:T(8,128)(2,1)} %bitcast.273), kind=kLoop, calls=%fused_computation.7 | loop fusion | flops 4194304 | bytes 16777216 | tf_op jit(solution)/shard_map/stack | solution.py:795
  244.3 14.4 %convolution_convert_fusion = bf16[2048,2176]{1,0:T(8,128)(2,1)} fusion(bf16[1024,2048]{1,0:T(8,128)(2,1)S(1)} %bitcast.269, bf16[1024,2176]{0,1:T(8,128)(2,1)} %copy-done.28), kind=kOutput, calls=%fused_computation.6 | convolution fusion | flops 9131261952 | bytes 17563648 | tf_op jit(solution)/shard_map/dot_general | solution.py:790
  258.6 82.3 %shard_map.467 = (f32[2,64,2176]{2,1,0:T(8,128)}, f32[2,64,1024]{2,1,0:T(8,128)}, f32[2,128,2048]{2,1,0:T(8,128)}) custom-call(bf16[2,4,4,64,2176]{4,3,2,1,0:T(8,128)(2,1)} %bitcast.261, bf16[2,4,4,64,1024]{4,3,2,1,0:T(8,128)(2,1)} %bitcast.272, bf16[2,2,2,2,128,2048]{5,4,3,2,1,0:T(8,128)(2,1)} %pad_maximum_fusion.branch), custom_call_target="tpu_custom_call" | custom-call | tf_op jit(solution)/shard_map/pallas_call | solution.py:486
  346.1 3.5 fusion.10
  361.2 17.8 %shard_map.468 = f32[8,640]{1,0:T(8,128)} custom-call(f32[8,640]{1,0:T(8,128)} %select_maximum_fusion.item), custom_call_target="tpu_custom_call" | custom-call | tf_op jit(solution)/shard_map/pallas_call | solution.py:570
  (287 shorter events, 106.7 us)
Async XLA Ops:
  0.7 394.7 %copy-start = (f32[12,128,128]{2,1,0:T(8,128)S(1)}, f32[12,128,128]{2,1,0:T(8,128)}, u32[]{:S(2)}) copy-start(f32[12,128,128]{2,1,0:T(8,128)} %param.53) | copy-start | bytes 2359300
  0.7 11.9 %copy-start.22 = (f32[64,1536]{1,0:T(8,128)S(1)}, f32[64,1536]{1,0:T(8,128)}, u32[]{:S(2)}) copy-start(f32[64,1536]{1,0:T(8,128)} %param.38) | copy-start | bytes 1179652
  0.7 13.0 %copy-start.64 = (bf16[128,2048]{1,0:T(8,128)(2,1)S(1)}, bf16[128,2048]{1,0:T(8,128)(2,1)}, u32[]{:S(2)}) copy-start(bf16[128,2048]{1,0:T(8,128)(2,1)} %param.32) | copy-start | bytes 1572868
  0.7 13.0 %copy-start.65 = (bf16[128,2048]{1,0:T(8,128)(2,1)S(1)}, bf16[128,2048]{1,0:T(8,128)(2,1)}, u32[]{:S(2)}) copy-start(bf16[128,2048]{1,0:T(8,128)(2,1)} %param.31) | copy-start | bytes 1572868
  5.9 11.2 %copy-start.59 = (s32[2048]{0:T(1024)}, s32[2048]{0:T(1024)S(1)}, u32[]{:S(2)}) copy-start(s32[2048]{0:T(1024)S(1)} %add.180) | copy-start | bytes 24580
  7.5 10.0 %copy-start.49 = (f32[2048]{0:T(1024)}, f32[2048]{0:T(1024)S(1)}, u32[]{:S(2)}) copy-start(f32[2048]{0:T(1024)S(1)} %mul.453) | copy-start | bytes 24580
  17.2 84.9 %copy-start.55 = (f32[128]{0:T(128)}, f32[128]{0:T(128)S(1)}, u32[]{:S(2)}) copy-start(f32[128]{0:T(128)S(1)} %broadcast_multiply_fusion.5) | copy-start | bytes 1540
  17.5 84.6 %copy-start.61 = (f32[128]{0:T(128)}, f32[128]{0:T(128)S(1)}, u32[]{:S(2)}) copy-start(f32[128]{0:T(128)S(1)} %add_rsqrt_fusion) | copy-start | bytes 1540
  193.3 9.5 %copy-start.29 = (bf16[1024,256]{1,0:T(8,128)(2,1)S(1)}, bf16[1024,256]{1,0:T(8,128)(2,1)}, u32[]{:S(2)}) copy-start(bf16[1024,256]{1,0:T(8,128)(2,1)} %reshape.347) | copy-start | bytes 1572868
  193.3 9.5 %copy-start.48 = (bf16[1024,64]{1,0:T(8,128)(2,1)S(1)}, bf16[1024,64]{1,0:T(8,128)(2,1)}, u32[]{:S(2)}) copy-start(bf16[1024,64]{1,0:T(8,128)(2,1)} %copy.227) | copy-start | bytes 393220
  193.3 9.5 %copy-start.58 = (bf16[1024]{0:T(1024)(128)(2,1)S(1)}, bf16[1024]{0:T(1024)(128)(2,1)}, u32[]{:S(2)}) copy-start(bf16[1024]{0:T(1024)(128)(2,1)} %copy-done.57) | copy-start | bytes 6148
  193.3 16.3 %slice-start.1 = ((s8[8388608]{0:T(1024)(128)(4,1)}), s8[4194304]{0:T(1024)(128)(4,1)S(1)}, s32[]{:S(2)}) async-start(s8[8388608]{0:T(1024)(128)(4,1)} %bitcast.262), calls=%async_computation.1 | async-start | bytes 8388608
  221.0 15.5 %copy-start.28 = (bf16[1024,2176]{0,1:T(8,128)(2,1)}, bf16[1024,2176]{0,1:T(8,128)(2,1)S(1)}, u32[]{:S(2)}) copy-start(bf16[1024,2176]{0,1:T(8,128)(2,1)S(1)} %fusion.80) | copy-start | bytes 13369348
  258.6 83.6 %copy-start.2 = (f32[256,2048]{1,0:T(8,128)S(1)}, f32[256,2048]{1,0:T(8,128)}, u32[]{:S(2)}) copy-start(f32[256,2048]{1,0:T(8,128)} %copy-done.1) | copy-start | bytes 6291460
  258.6 83.7 %copy-start.50 = (f32[2048]{0:T(1024)S(1)}, f32[2048]{0:T(1024)}, u32[]{:S(2)}) copy-start(f32[2048]{0:T(1024)} %copy-done.49) | copy-start | bytes 24580
  258.6 83.7 %copy-start.56 = (f32[128]{0:T(128)S(1)}, f32[128]{0:T(128)}, u32[]{:S(2)}) copy-start(f32[128]{0:T(128)} %copy-done.55) | copy-start | bytes 1540
  258.6 83.7 %copy-start.62 = (f32[128]{0:T(128)S(1)}, f32[128]{0:T(128)}, u32[]{:S(2)}) copy-start(f32[128]{0:T(128)} %copy-done.61) | copy-start | bytes 1540
  360.0 29.4 %copy-start.53 = (f32[2,2048]{1,0:T(2,128)S(1)}, f32[2,2048]{1,0:T(2,128)}, u32[]{:S(2)}) copy-start(f32[2,2048]{1,0:T(2,128)} %param.35) | copy-start | bytes 49156
  360.2 40.3 %copy-start.31 = (f32[64,512]{1,0:T(8,128)S(1)}, f32[64,512]{1,0:T(8,128)}, u32[]{:S(2)}) copy-start(f32[64,512]{1,0:T(8,128)} %param.39) | copy-start | bytes 393220
  360.2 41.0 %copy-start.15 = (f32[64,1408]{1,0:T(8,128)S(1)}, f32[64,1408]{1,0:T(8,128)}, u32[]{:S(2)}) copy-start(f32[64,1408]{1,0:T(8,128)} %concatenate.92) | copy-start | bytes 1081348
  387.4 15.3 %copy-start.14 = (f32[64,1408]{1,0:T(8,128)S(1)}, f32[64,1408]{1,0:T(8,128)}, u32[]{:S(2)}) copy-start(f32[64,1408]{1,0:T(8,128)} %concatenate.93) | copy-start | bytes 1081348
  387.4 15.3 %copy-start.18 = (f32[11,128,128]{2,1,0:T(8,128)S(1)}, f32[11,128,128]{2,1,0:T(8,128)}, u32[]{:S(2)}) copy-start(f32[11,128,128]{2,1,0:T(8,128)} %param.56) | copy-start | bytes 2162692
  389.4 14.1 %copy-start.54 = (f32[2,2048]{1,0:T(2,128)}, f32[2,2048]{1,0:T(2,128)S(1)}, u32[]{:S(2)}) copy-start(f32[2,2048]{1,0:T(2,128)S(1)} %mul.512) | copy-start | bytes 49156
  392.5 11.8 %copy-start.17 = (f32[11,128,128]{2,1,0:T(8,128)S(1)}, f32[11,128,128]{2,1,0:T(8,128)}, u32[]{:S(2)}) copy-start(f32[11,128,128]{2,1,0:T(8,128)} %param.57) | copy-start | bytes 2162692
  (45 other events, 220.4 us)
